TPU v7x, 32 devices: a whole 2x2x4 slice. The times are simulated.
32 devices in a mesh: mp: 2 (over x), blk: 8 (over z, y), tok: 2 (over core).
Axes of the slice: x: 2, y: 2, z: 4, core: 2. Of those that a mesh axis runs over, the one named last changes fastest.
Arguments:
- inputs: bfloat16 [2, 256, 28672], P('mp', 'tok', 'blk'), may hold values from -1.1953125 to 1.1953125
- down_weight: bfloat16 [2, 512, 28672], P('mp', None, 'blk'), may hold values from -0.03125 to 0.03125
Outputs:
- denominator: float32 [256, 28672], P('blk', 'tok')
- numerator: float32 [256, 512], P('blk', 'tok')
All inputs are finite; a program needn't handle non-finite values.
Results may differ from a plain program's by a relative error of at most 0.0003.
Values may be sent and summed in bfloat16 or wider, within the bound.
A program may use at most 64 MiB of HBM per device.

v0:
```python
import jax
import jax.numpy as jnp
from jax import lax
from jax.sharding import PartitionSpec as P

DIN = 28672
COLS = 512
ROW_DEV = 32


OFF_SCALE = 0.9


def local(inputs, down_weight):
    x_local = inputs[0]
    w_local = down_weight[0]
    span_width = x_local.shape[1]
    x_rows = x_local[:, :ROW_DEV]
    blk_index = lax.axis_index("blk")
    tok_index = lax.axis_index("tok")
    tok_count = lax.axis_size("tok")
    col_share = DIN // tok_count
    col_parts = COLS // tok_count
    partial_value = lax.dot_general(
        x_rows,
        lax.all_gather(x_local, "blk", axis=1, tiled=True),
        (((0,), (0,)), ((), ())),
        preferred_element_type=jnp.float32,
    )
    gram_panel = lax.psum(partial_value, "tok")
    col_ids = lax.broadcasted_iota(jnp.int32, gram_panel.shape, 1)
    row_ids = lax.broadcasted_iota(jnp.int32, gram_panel.shape, 0)
    on_diag = col_ids == blk_index * span_width + row_ids
    reduced = jnp.where(on_diag, gram_panel, OFF_SCALE * gram_panel)
    denominator = lax.dynamic_slice_in_dim(reduced, tok_index * col_share, col_share, 1)
    w_group = lax.dynamic_slice_in_dim(w_local, tok_index * col_parts, col_parts, 0)
    numerator = lax.dot_general(
        reduced,
        lax.all_gather(w_group, "blk", axis=1, tiled=True).astype(jnp.float32),
        (((1,), (1,)), ((), ())),
        precision=lax.Precision.HIGHEST,
        preferred_element_type=jnp.float32,
    )
    denominator, numerator = lax.psum((denominator, numerator), "mp")
    return (denominator, numerator)


def solution(mesh):
    placed = (P("mp", "tok", "blk"), P("mp", None, "blk"))
    return jax.shard_map(
        local,
        mesh=mesh,
        in_specs=placed,
        out_specs=(P("blk", "tok"), P("blk", "tok")),
        check_vma=False,
    )
```

profile of v0, /device:TPU:1, one launch (start us, length us, event | category | flops | bytes accessed | tf_op | source)
XLA Modules:
  0.0 426.9 jit_solution(528568240312132951)
XLA Ops:
  7.2 0.0 all-gather.5.cloned.1.call-start
  7.2 0.7 all-gather.5.cloned.1.call-update
  7.9 0.0 all-reduce.3.cloned.1.call-start
  7.9 116.0 %all-gather.5.cloned.1.call-done = bf16[1,128,28672]{2,1,0:T(8,128)(2,1)} async-done(((bf16[1,128,3584]{2,1,0:T(8,128)(2,1)}), bf16[1,128,28672]{2,1,0:T(8,128)(2,1)}) %all-gather.5.cloned.1.call-update) | async-done | bytes 7340048 | tf_op jit(solution)/shard_map/all_gather | solution.py:26
  123.9 6.0 %fusion.2 = f32[32,28672]{1,0:T(8,128)} fusion(bf16[1,128,28672]{2,1,0:T(8,128)(2,1)} %all-gather.5.cloned.1.call-done, bf16[128,3584]{1,0:T(8,128)(2,1)} %bitcast.8), kind=kOutput, calls=%fused_computation.2 | convolution fusion | flops 234881024 | bytes 11042816 | tf_op jit(solution)/shard_map/dot_general | solution.py:24
  129.9 0.0 all-reduce.3.cloned.1.call-update
  130.0 0.0 all-gather.7.cloned.1.call-start
  130.0 2.9 constant_dynamic-slice_fusion
  132.9 0.0 all-gather.7.cloned.1.call-update
  132.9 0.0 all-reduce.5.cloned.1.call-start
  133.0 20.3 %all-reduce.3.cloned.1.call-done = f32[32,28672]{1,0:T(8,128)} async-done(((f32[32,28672]{1,0:T(8,128)}), f32[32,28672]{1,0:T(8,128)}) %all-reduce.3.cloned.1.call-update) | async-done | bytes 3670032 | tf_op jit(solution)/shard_map/psum | solution.py:30
  153.3 2.5 multiply_select_fusion
  155.8 0.0 copy-start
  155.8 1.8 copy-done
  157.6 1.3 constant_dynamic-slice_fusion.1
  159.0 0.0 all-reduce.5.cloned.1.call-update
  159.0 199.2 %all-gather.7.cloned.1.call-done = bf16[1,256,28672]{2,1,0:T(8,128)(2,1)} async-done(((bf16[1,256,3584]{2,1,0:T(8,128)(2,1)}), bf16[1,256,28672]{2,1,0:T(8,128)(2,1)}) %all-gather.7.cloned.1.call-update) | async-done | bytes 14680080 | tf_op jit(solution)/shard_map/all_gather | solution.py:39
  358.2 16.5 %fusion = f32[32,256]{1,0:T(8,128)S(1)} fusion(f32[32,28672]{1,0:T(8,128)} %copy-done, bf16[1,256,28672]{2,1,0:T(8,128)(2,1)} %all-gather.7.cloned.1.call-done), kind=kOutput, calls=%fused_computation | convolution fusion | flops 2818572288 | bytes 18382848 | tf_op jit(solution)/shard_map/dot_general | solution.py:37
  374.6 8.3 %psum.23 = f32[32,256]{1,0:T(8,128)} all-reduce(f32[32,256]{1,0:T(8,128)S(1)} %fusion), channel_id=1, replica_groups=mesh['mp'=2,'blk'=8,'tok'=2] {'mp'}, use_global_device_ids=true, to_apply=%region_2.3 | all-reduce | flops 8192 | bytes 65536 | tf_op jit(solution)/shard_map/psum | solution.py:44
  383.0 34.5 %all-reduce.5.cloned.1.call-done = f32[32,14336]{1,0:T(8,128)} async-done(((f32[32,14336]{1,0:T(8,128)}), f32[32,14336]{1,0:T(8,128)}) %all-reduce.5.cloned.1.call-update) | async-done | bytes 1835024 | tf_op jit(solution)/shard_map/psum | solution.py:44
  417.5 2.8 copy.6
  (1 shorter events, 0.0 us)
Async XLA Ops:
  7.2 116.7 %all-gather.5.cloned.1.call-start = ((), (), s32[]{:S(2)}) async-start(), calls=%async_computation.2 | async-start | bytes 8257536 | tf_op jit(solution)/shard_map/all_gather | solution.py:26
  7.9 145.4 %all-reduce.3.cloned.1.call-start = ((), (), s32[]{:S(2)}) async-start(), calls=%async_computation | async-start | bytes 7340032 | tf_op jit(solution)/shard_map/psum | solution.py:30
  130.0 228.2 %all-gather.7.cloned.1.call-start = ((), (), s32[]{:S(2)}) async-start(), calls=%async_computation.3 | async-start | bytes 16515072 | tf_op jit(solution)/shard_map/all_gather | solution.py:39
  132.9 284.6 %all-reduce.5.cloned.1.call-start = ((), (), s32[]{:S(2)}) async-start(), calls=%async_computation.1 | async-start | bytes 3670016 | tf_op jit(solution)/shard_map/psum | solution.py:44
  155.8 1.8 copy-start
Sparse Core Ops, SparseCore 0:
  10.2 113.6 all-gather.4
  130.1 23.1 all-reduce.2
  155.7 202.3 all-gather.6
  361.0 56.4 all-reduce.4
where the time goes:
time: 428 us; the launch traced here: 427 us
  waiting for transfers between devices  371 us (87%)
  matrix products  22.5 us (5%)
  between operations  13.8 us (3%)
  local copies, waits for them, and re-layouts  8.87 us (2%)
  blocking collectives  8.35 us (2%)
    all_gather x1, waiting for transfers between devices, local(): lax.all_gather(w_group, 'blk', axis=1, tiled=True).astype(jnp.float32)  199 us
    all_gather x1, waiting for transfers between devices, local(): lax.all_gather(x_local, 'blk', axis=1, tiled=True)  116 us
    psum x1, waiting for transfers between devices, local(): denominator, numerator = lax.psum((denominator, numerator), 'mp')  34.5 us
    psum x1, waiting for transfers between devices, local(): gram_panel = lax.psum(partial_value, 'tok')  20.3 us
    dot_general x1, matrix products, local(): lax.dot_general(reduced, lax.all_gather(w_group, 'blk', axis=1, tiled=Tru...  16.5 us
  transfers between devices with their start and end apart: 4, of which 4 were waited for; matrix products, arithmetic and copies ran while one was open for 5% of the time, Pallas kernels for 0%

commit v1 on v0

v1 whole, which is shorter than its diff:
```python
import functools

import jax
import jax.numpy as jnp
from jax import lax
from jax.experimental import pallas as pl
from jax.experimental.pallas import tpu as pltpu
from jax.sharding import PartitionSpec as P

ROW_DEV = 32
OFF_SCALE = 0.9
LANE = 128
MESH = pl.DeviceIdType.MESH


def ds(start, size):
    return pl.ds(pl.multiple_of(start, size), size)


def lanes(start, size):
    return pl.ds(pl.multiple_of(start, LANE), size)


def kernel(
    nb, chunks,
    x_hbm, w_hbm, den, num,
    xv, wv, xq, xwt, g, nloc, n_a, n_s, n_b, n_t, n_c,
    ld, xs_send, xs_recv, s1_send, s1_recv, s2_send, s2_recv,
    p_send, p_recv, f_send, f_recv, a_sem, b_sem, c_send, c_recv, d_sem,
):
    m, b, t = lax.axis_index("mp"), lax.axis_index("blk"), lax.axis_index("tok")
    toks, span = xv.shape
    cols = wv.shape[0]
    quarter = span // 4
    per_half = nb // 2
    s = m * 2 + t
    om, ot = 1 - m, 1 - t
    group = [(om, t), (om, ot), (m, ot)]

    load_x = pltpu.make_async_copy(x_hbm, xv, ld.at[0])
    load_w = pltpu.make_async_copy(w_hbm, wv, ld.at[1])
    load_q = pltpu.make_async_copy(
        x_hbm.at[:, lanes(s * quarter, quarter)], xq.at[ds(s * toks, toks), :], ld.at[2]
    )
    load_x.start()
    load_w.start()
    load_q.start()

    barrier = pltpu.get_barrier_semaphore()
    peers = [(om, b, t), (om, b, ot), (m, b, ot)]
    for k in range(1, nb):
        bp = lax.rem(b + k, nb)
        peers += [(m, bp, t), (m, bp, ot)]
    for peer in peers:
        pl.semaphore_signal(barrier, inc=1, device_id=peer, device_id_type=MESH)
    pl.semaphore_wait(barrier, len(peers))

    def remote(src, dst, send, recv, device):
        return pltpu.make_async_remote_copy(
            src_ref=src, dst_ref=dst, send_sem=send, recv_sem=recv,
            device_id=device, device_id_type=MESH,
        )

    sent = []

    exchange = []
    for c, (off, width) in enumerate(chunks):
        copies = []
        for k, (pm, pt) in enumerate(group):
            ps = pm * 2 + pt
            copies.append(remote(
                x_hbm.at[:, lanes(ps * quarter + off, width)],
                xq.at[ds(s * toks, toks), off:off + width],
                xs_send.at[c, k], xs_recv.at[c, k], (pm, b, pt),
            ))
        for cp in copies:
            cp.start()
        exchange.append(copies)
        sent += copies

    load_x.wait()
    own_t = jnp.transpose(xv[:, :LANE].astype(jnp.float32))[:ROW_DEV]
    xwt[ds(b * ROW_DEV, ROW_DEV), lanes(s * toks, toks)] = own_t.astype(jnp.bfloat16)
    stage1 = []
    for k in range(1, nb):
        bp = lax.rem(b + k, nb)
        piece = xwt.at[ds(b * ROW_DEV, ROW_DEV), lanes(s * toks, toks)]
        cp = remote(piece, piece, s1_send.at[k], s1_recv.at[k], (m, bp, t))
        cp.start()
        stage1.append(cp)
    sent += stage1

    load_w.wait()
    z = lax.dot_general(
        xv[...], wv[...], (((1,), (1,)), ((), ())), preferred_element_type=jnp.float32
    )
    z_hi = z.astype(jnp.bfloat16)
    z_lo = (z - z_hi.astype(jnp.float32)).astype(jnp.bfloat16)
    w_t = jnp.transpose(wv[:, :LANE].astype(jnp.float32))[:ROW_DEV]
    diag = jnp.sum(own_t * own_t, axis=1, keepdims=True)

    for cp in stage1:
        cp.wait_recv()
    stage2 = []
    for k, (pm, pt) in enumerate(group):
        piece = xwt.at[:, lanes(s * toks, toks)]
        cp = remote(piece, piece, s2_send.at[k], s2_recv.at[k], (pm, b, pt))
        cp.start()
        stage2.append(cp)
    sent += stage2

    rows_t = xwt[:, lanes(s * toks, toks)]
    nloc[...] = OFF_SCALE * (
        jnp.dot(rows_t, z_hi, preferred_element_type=jnp.float32)
        + jnp.dot(rows_t, z_lo, preferred_element_type=jnp.float32)
    )
    mine = ds(b * ROW_DEV, ROW_DEV)
    nloc[mine, :] = nloc[mine, :] + (1.0 - OFF_SCALE) * diag * w_t
    half, part = cols // 2, cols // 4
    copy_a = remote(
        nloc.at[:, lanes(ot * half, half)], n_a, a_sem.at[0], a_sem.at[1], (m, b, ot)
    )
    copy_a.start()
    sent.append(copy_a)
    copy_a.wait_recv()
    n_s[...] = nloc[:, lanes(t * half, half)] + n_a[...]
    copy_b = remote(
        n_s.at[:, lanes(om * part, part)], n_b, b_sem.at[0], b_sem.at[1], (om, b, t)
    )
    copy_b.start()
    sent.append(copy_b)

    owner = b // per_half
    base = lax.rem(b, per_half) * span + s * quarter
    slot = lax.rem(b, per_half) * 2 + t
    load_q.wait()
    for c, (off, width) in enumerate(chunks):
        for cp in exchange[c]:
            cp.wait_recv()
        if c == 0:
            for cp in stage2:
                cp.wait_recv()
        gram = jnp.dot(
            xwt[...], xq[:, off:off + width], preferred_element_type=jnp.float32
        )
        if off == 0:
            row_ids = lax.broadcasted_iota(jnp.int32, gram.shape, 0)
            col_ids = lax.broadcasted_iota(jnp.int32, gram.shape, 1)
            first = jnp.where(s == 0, ROW_DEV, 0)
            on_diag = (col_ids < first) & (row_ids == b * ROW_DEV + col_ids)
            g[:, off:off + width] = jnp.where(on_diag, gram, OFF_SCALE * gram)
        else:
            g[:, off:off + width] = OFF_SCALE * gram
        for k in list(range(1, nb)) + [0]:
            bp = lax.rem(b + k, nb)
            src = g.at[ds(bp * ROW_DEV, ROW_DEV), off:off + width]
            dst = den.at[:, lanes(base + off, width)]
            cp = remote(src, dst, p_send.at[c, k], p_recv.at[c, slot], (m, bp, owner))
            if k:
                cp.start()
                sent.append(cp)
            else:
                here = pltpu.make_async_copy(src, dst, p_recv.at[c, slot])
                pl.when(owner == t)(here.start)
                pl.when(owner != t)(cp.start)

    copy_b.wait_recv()
    n_t[...] = n_s[:, lanes(m * part, part)] + n_b[...]
    stage_c = []
    for k in range(1, nb):
        bp = lax.rem(b + k, nb)
        cp = remote(
            n_t.at[ds(bp * ROW_DEV, ROW_DEV), :], n_c.at[k],
            c_send.at[k], c_recv.at[k], (m, bp, t),
        )
        cp.start()
        stage_c.append(cp)
    sent += stage_c

    forwards = []
    for c, (off, width) in enumerate(chunks):
        for j in range(nb):
            i = lax.rem(lax.rem(b, per_half) + (nb - j // 2), per_half)
            core = j % 2
            where = i * 2 + core
            came = den.at[:, lanes(i * span + (m * 2 + core) * quarter + off, width)]
            remote(
                came, came, f_send.at[c, j], p_recv.at[c, where], (om, b, t)
            ).wait_recv()
            cp = remote(came, came, f_send.at[c, j], f_recv.at[c, j], (om, b, t))
            cp.start()
            forwards.append(cp)
        if c == 0:
            total = n_t[mine, :]
            for k, cp in enumerate(stage_c):
                cp.wait_recv()
                total = total + n_c[k + 1]
            num[:, lanes(m * part, part)] = total
            piece = num.at[:, lanes(m * part, part)]
            copy_d = remote(piece, piece, d_sem.at[0], d_sem.at[1], (om, b, t))
            copy_d.start()
            sent.append(copy_d)
    copy_d.wait_recv()
    for cp in forwards:
        cp.wait_recv()
    for cp in sent + forwards:
        cp.wait_send()
    for c, (off, width) in enumerate(chunks):
        src = g.at[ds(b * ROW_DEV, ROW_DEV), off:off + width]
        dst = den.at[:, lanes(base + off, width)]
        cp = remote(src, dst, p_send.at[c, 0], p_recv.at[c, slot], (m, b, ot))
        pl.when(owner != t)(cp.wait_send)


def fused(x, w, nb):
    toks, span = x.shape
    cols = w.shape[0]
    rows = nb * ROW_DEV
    quarter = span // 4
    first = (quarter // LANE + 1) // 2 * LANE
    chunks = [(0, first), (first, quarter - first)]
    nc = len(chunks)
    dma = pltpu.SemaphoreType.DMA
    f32, bf16 = jnp.float32, jnp.bfloat16
    return pl.pallas_call(
        functools.partial(kernel, nb, chunks),
        out_shape=(
            jax.ShapeDtypeStruct((ROW_DEV, nb * span // 2), f32),
            jax.ShapeDtypeStruct((ROW_DEV, cols // 2), f32),
        ),
        in_specs=[pl.BlockSpec(memory_space=pl.ANY)] * 2,
        out_specs=(pl.BlockSpec(memory_space=pltpu.VMEM),) * 2,
        scratch_shapes=[
            pltpu.VMEM((toks, span), bf16),
            pltpu.VMEM((cols, span), bf16),
            pltpu.VMEM((4 * toks, quarter), bf16),
            pltpu.VMEM((rows, 4 * toks), bf16),
            pltpu.VMEM((rows, quarter), f32),
            pltpu.VMEM((rows, cols), f32),
            pltpu.VMEM((rows, cols // 2), f32),
            pltpu.VMEM((rows, cols // 2), f32),
            pltpu.VMEM((rows, cols // 4), f32),
            pltpu.VMEM((rows, cols // 4), f32),
            pltpu.VMEM((nb, ROW_DEV, cols // 4), f32),
            dma((3,)),
            dma((nc, 3)), dma((nc, 3)),
            dma((nb,)), dma((nb,)),
            dma((3,)), dma((3,)),
            dma((nc, nb)), dma((nc, nb)),
            dma((nc, nb)), dma((nc, nb)),
            dma((2,)), dma((2,)),
            dma((nb,)), dma((nb,)),
            dma((2,)),
        ],
        compiler_params=pltpu.CompilerParams(
            collective_id=0, has_side_effects=True, vmem_limit_bytes=40 * 1024 * 1024
        ),
        cost_estimate=pl.CostEstimate(
            flops=2 * toks * span * cols + 2 * rows * quarter * 4 * toks,
            bytes_accessed=2 * (toks + cols) * span + 2 * ROW_DEV * nb * span,
            transcendentals=0,
        ),
    )(x, w)


def general(x, w, din):
    x_rows = x[:, :ROW_DEV]
    span = x.shape[1]
    b, t, nt = lax.axis_index("blk"), lax.axis_index("tok"), lax.axis_size("tok")
    share, part = din // nt, w.shape[0] // nt
    gram = lax.psum(
        lax.dot_general(
            x_rows, lax.all_gather(x, "blk", axis=1, tiled=True),
            (((0,), (0,)), ((), ())), preferred_element_type=jnp.float32,
        ),
        "tok",
    )
    col_ids = lax.broadcasted_iota(jnp.int32, gram.shape, 1)
    row_ids = lax.broadcasted_iota(jnp.int32, gram.shape, 0)
    reduced = jnp.where(col_ids == b * span + row_ids, gram, OFF_SCALE * gram)
    den = lax.dynamic_slice_in_dim(reduced, t * share, share, 1)
    w_group = lax.dynamic_slice_in_dim(w, t * part, part, 0)
    num = lax.dot_general(
        reduced, lax.all_gather(w_group, "blk", axis=1, tiled=True).astype(jnp.float32),
        (((1,), (1,)), ((), ())), precision=lax.Precision.HIGHEST,
        preferred_element_type=jnp.float32,
    )
    return lax.psum((den, num), "mp")


def solution(mesh):
    nm, nb, nt = mesh.shape["mp"], mesh.shape["blk"], mesh.shape["tok"]

    def local(inputs, down_weight):
        x, w = inputs[0], down_weight[0]
        toks, span = x.shape
        fits = (
            nm == 2 and nt == 2 and nb % 2 == 0 and toks == LANE
            and span % (4 * LANE) == 0 and span >= 8 * LANE
            and w.shape[0] % (4 * LANE) == 0
        )
        if fits:
            return fused(x, w, nb)
        return general(x, w, nb * span)

    return jax.shard_map(
        local,
        mesh=mesh,
        in_specs=(P("mp", "tok", "blk"), P("mp", None, "blk")),
        out_specs=(P("blk", "tok"), P("blk", "tok")),
        check_vma=False,
    )
```

time: 428 us -> 62.5 us (0.15)
  waiting for transfers between devices: 371 us -> 0 us
  Pallas kernels: 0 us -> 55.8 us
  matrix products: 22.5 us -> 0 us
  between operations: 13.8 us -> 0.65 us
  blocking collectives: 8.35 us -> 0 us
    all_gather x2 -> x0, waiting for transfers between devices: 315 us -> none  [the longest x1 199 us: local(): lax.all_gather(w_group, 'blk', axis=1, tiled=True).astype(jnp.float32)]
    pallas_call x0 -> x1, Pallas kernels: none -> 55.8 us  [fused(): pl.pallas_call(functools.partial(kernel, nb, chunks), out_shape=(jax.Shap...]
    psum x2 -> x0, waiting for transfers between devices: 54.8 us -> none  [the longest x1 34.5 us: local(): denominator, numerator = lax.psum((denominator, numerator), 'mp')]
    dot_general x2 -> x0, matrix products: 22.5 us -> none  [the longest x1 16.5 us: local(): lax.dot_general(reduced, lax.all_gather(w_group, 'blk', axis=1, tiled=Tru...]
    psum x1 -> x0, blocking collectives: 8.35 us -> none  [local(): denominator, numerator = lax.psum((denominator, numerator), 'mp')]
  transfers between devices with their start and end apart: 4 -> 0, of which waited for: 4 -> 0; matrix products, arithmetic and copies ran while one was open for 5% -> 0% of each run, Pallas kernels for 0% -> 0%
where the time goes in v1:
time: 62.5 us; the launch traced here: 61.5 us
  Pallas kernels  55.8 us (89%)
  local copies, waits for them, and re-layouts  5.06 us (8%)
  between operations  0.65 us (1%)
    pallas_call x1, Pallas kernels, fused(): pl.pallas_call(functools.partial(kernel, nb, chunks), out_shape=(jax.Shap...  55.8 us
    unnamed x6, local copies, waits for them, and re-layouts  5.06 us

profile of v1, /device:TPU:1, one launch (start us, length us, event | category | flops | bytes accessed | tf_op | source)
XLA Modules:
  0.0 61.5 jit_solution(6311804902998541073)
XLA Ops:
  0.6 0.0 copy-start
  0.6 2.0 %copy-done = bf16[1,512,3584]{2,1,0:T(8,128)(2,1)S(1)} copy-done((bf16[1,512,3584]{2,1,0:T(8,128)(2,1)S(1)}, bf16[1,512,3584]{2,1,0:T(8,128)(2,1)}, u32[]{:S(2)}) %copy-start) | copy-done | bytes 3670040
  2.7 0.0 copy-start.1
  2.7 1.2 %copy-done.1 = bf16[1,128,3584]{2,1,0:T(8,128)(2,1)S(1)} copy-done((bf16[1,128,3584]{2,1,0:T(8,128)(2,1)S(1)}, bf16[1,128,3584]{2,1,0:T(8,128)(2,1)}, u32[]{:S(2)}) %copy-start.1) | copy-done | bytes 917528
  3.8 55.8 %shard_map.41 = (f32[32,14336]{1,0:T(8,128)S(1)}, f32[32,256]{1,0:T(8,128)S(1)}) custom-call(bf16[128,3584]{1,0:T(8,128)(2,1)S(1)} %bitcast.3, bf16[512,3584]{1,0:T(8,128)(2,1)S(1)} %bitcast.2), custom_call_target="tpu_custom_call" | custom-call | flops 704643072 | bytes 6422528 | tf_op jit(solution)/shard_map/pallas_call | solution.py:225
  59.6 1.2 %copy.6 = f32[32,14336]{1,0:T(8,128)} copy(f32[32,14336]{1,0:T(8,128)S(1)} %get-tuple-element.4) | data formatting | bytes 3670016
  60.9 0.6 copy.7
Async XLA Ops:
  0.6 2.0 %copy-start = (bf16[1,512,3584]{2,1,0:T(8,128)(2,1)S(1)}, bf16[1,512,3584]{2,1,0:T(8,128)(2,1)}, u32[]{:S(2)}) copy-start(bf16[1,512,3584]{2,1,0:T(8,128)(2,1)} %param.3) | copy-start | bytes 11010052
  2.7 1.2 %copy-start.1 = (bf16[1,128,3584]{2,1,0:T(8,128)(2,1)S(1)}, bf16[1,128,3584]{2,1,0:T(8,128)(2,1)}, u32[]{:S(2)}) copy-start(bf16[1,128,3584]{2,1,0:T(8,128)(2,1)} %param.2) | copy-start | bytes 2752516

commit v2 on v1

--- a/solution.py
+++ b/solution.py
@@ -24,9 +24,9 @@
 def kernel(
     nb, chunks,
     x_hbm, w_hbm, den, num,
-    xv, wv, xq, xwt, g, nloc, n_a, n_s, n_b, n_t, n_c,
+    xv, wv, xq, xwt, g, nloc, n_a, n_s, n_c, n_t, n_d,
     ld, xs_send, xs_recv, s1_send, s1_recv, s2_send, s2_recv,
-    p_send, p_recv, f_send, f_recv, a_sem, b_sem, c_send, c_recv, d_sem,
+    p_send, p_recv, f_send, f_recv, a_sem, c_send, c_recv, d_sem,
 ):
     m, b, t = lax.axis_index("mp"), lax.axis_index("blk"), lax.axis_index("tok")
     toks, span = xv.shape
@@ -62,6 +62,9 @@
         )
 
     sent = []
+
+    def piece_t(rows, sm, st):
+        return xwt.at[rows, lanes((sm * 2 + st) * toks, toks)]
 
     exchange = []
     for c, (off, width) in enumerate(chunks):
@@ -73,73 +76,56 @@
                 xq.at[ds(s * toks, toks), off:off + width],
                 xs_send.at[c, k], xs_recv.at[c, k], (pm, b, pt),
             ))
+        exchange.append(copies)
+        sent += copies
+    for cp in exchange[0]:
+        cp.start()
+
+    load_x.wait()
+    mine = ds(b * ROW_DEV, ROW_DEV)
+    own_t = jnp.transpose(xv[:, :LANE].astype(jnp.float32))[:ROW_DEV]
+    xwt[mine, lanes(s * toks, toks)] = own_t.astype(jnp.bfloat16)
+    over_x = remote(
+        piece_t(mine, m, t), piece_t(mine, m, t), d_sem.at[2], d_sem.at[3], (om, b, t)
+    )
+    over_x.start()
+    stage1 = []
+    for r in range(2):
+        copies = []
+        for k in range(1, nb):
+            bp = lax.rem(b + k, nb)
+            piece = piece_t(mine, om if r else m, t)
+            cp = remote(piece, piece, s1_send.at[r, k], s1_recv.at[r, k], (m, bp, t))
+            copies.append(cp)
+        if r:
+            over_x.wait_recv()
         for cp in copies:
             cp.start()
-        exchange.append(copies)
-        sent += copies
-
-    load_x.wait()
-    own_t = jnp.transpose(xv[:, :LANE].astype(jnp.float32))[:ROW_DEV]
-    xwt[ds(b * ROW_DEV, ROW_DEV), lanes(s * toks, toks)] = own_t.astype(jnp.bfloat16)
-    stage1 = []
-    for k in range(1, nb):
-        bp = lax.rem(b + k, nb)
-        piece = xwt.at[ds(b * ROW_DEV, ROW_DEV), lanes(s * toks, toks)]
-        cp = remote(piece, piece, s1_send.at[k], s1_recv.at[k], (m, bp, t))
+        stage1.append(copies)
+    for cp in exchange[1]:
         cp.start()
-        stage1.append(cp)
-    sent += stage1
-
-    load_w.wait()
-    z = lax.dot_general(
-        xv[...], wv[...], (((1,), (1,)), ((), ())), preferred_element_type=jnp.float32
-    )
-    z_hi = z.astype(jnp.bfloat16)
-    z_lo = (z - z_hi.astype(jnp.float32)).astype(jnp.bfloat16)
-    w_t = jnp.transpose(wv[:, :LANE].astype(jnp.float32))[:ROW_DEV]
-    diag = jnp.sum(own_t * own_t, axis=1, keepdims=True)
-
-    for cp in stage1:
-        cp.wait_recv()
     stage2 = []
-    for k, (pm, pt) in enumerate(group):
-        piece = xwt.at[:, lanes(s * toks, toks)]
-        cp = remote(piece, piece, s2_send.at[k], s2_recv.at[k], (pm, b, pt))
+    for r in range(2):
+        for cp in stage1[r]:
+            cp.wait_recv()
+        piece = piece_t(slice(None), om if r else m, t)
+        cp = remote(piece, piece, s2_send.at[r], s2_recv.at[r], (m, b, ot))
         cp.start()
         stage2.append(cp)
-    sent += stage2
-
-    rows_t = xwt[:, lanes(s * toks, toks)]
-    nloc[...] = OFF_SCALE * (
-        jnp.dot(rows_t, z_hi, preferred_element_type=jnp.float32)
-        + jnp.dot(rows_t, z_lo, preferred_element_type=jnp.float32)
-    )
-    mine = ds(b * ROW_DEV, ROW_DEV)
-    nloc[mine, :] = nloc[mine, :] + (1.0 - OFF_SCALE) * diag * w_t
-    half, part = cols // 2, cols // 4
-    copy_a = remote(
-        nloc.at[:, lanes(ot * half, half)], n_a, a_sem.at[0], a_sem.at[1], (m, b, ot)
-    )
-    copy_a.start()
-    sent.append(copy_a)
-    copy_a.wait_recv()
-    n_s[...] = nloc[:, lanes(t * half, half)] + n_a[...]
-    copy_b = remote(
-        n_s.at[:, lanes(om * part, part)], n_b, b_sem.at[0], b_sem.at[1], (om, b, t)
-    )
-    copy_b.start()
-    sent.append(copy_b)
+    sent += [over_x] + stage1[0] + stage1[1] + stage2
 
     owner = b // per_half
     base = lax.rem(b, per_half) * span + s * quarter
     slot = lax.rem(b, per_half) * 2 + t
-    load_q.wait()
-    for c, (off, width) in enumerate(chunks):
+    half = cols // 2
+
+    def gram_chunk(c):
+        off, width = chunks[c]
         for cp in exchange[c]:
             cp.wait_recv()
-        if c == 0:
-            for cp in stage2:
-                cp.wait_recv()
+        if c + 2 < len(chunks):
+            for cp in exchange[c + 2]:
+                cp.start()
         gram = jnp.dot(
             xwt[...], xq[:, off:off + width], preferred_element_type=jnp.float32
         )
@@ -164,23 +150,12 @@
                 pl.when(owner == t)(here.start)
                 pl.when(owner != t)(cp.start)
 
-    copy_b.wait_recv()
-    n_t[...] = n_s[:, lanes(m * part, part)] + n_b[...]
-    stage_c = []
-    for k in range(1, nb):
-        bp = lax.rem(b + k, nb)
-        cp = remote(
-            n_t.at[ds(bp * ROW_DEV, ROW_DEV), :], n_c.at[k],
-            c_send.at[k], c_recv.at[k], (m, bp, t),
-        )
-        cp.start()
-        stage_c.append(cp)
-    sent += stage_c
-
     forwards = []
-    for c, (off, width) in enumerate(chunks):
+
+    def forward_chunk(c):
+        off, width = chunks[c]
         for j in range(nb):
-            i = lax.rem(lax.rem(b, per_half) + (nb - j // 2), per_half)
+            i = lax.rem(lax.rem(b, per_half) + (per_half - j // 2), per_half)
             core = j % 2
             where = i * 2 + core
             came = den.at[:, lanes(i * span + (m * 2 + core) * quarter + off, width)]
@@ -190,23 +165,68 @@
             cp = remote(came, came, f_send.at[c, j], f_recv.at[c, j], (om, b, t))
             cp.start()
             forwards.append(cp)
-        if c == 0:
-            total = n_t[mine, :]
-            for k, cp in enumerate(stage_c):
-                cp.wait_recv()
-                total = total + n_c[k + 1]
-            num[:, lanes(m * part, part)] = total
-            piece = num.at[:, lanes(m * part, part)]
-            copy_d = remote(piece, piece, d_sem.at[0], d_sem.at[1], (om, b, t))
-            copy_d.start()
-            sent.append(copy_d)
+
+    load_q.wait()
+    for cp in stage2:
+        cp.wait_recv()
+    gram_chunk(0)
+
+    load_w.wait()
+    z = lax.dot_general(
+        xv[...], wv[...], (((1,), (1,)), ((), ())), preferred_element_type=jnp.float32
+    )
+    z_hi = z.astype(jnp.bfloat16)
+    z_lo = (z - z_hi.astype(jnp.float32)).astype(jnp.bfloat16)
+    w_t = jnp.transpose(wv[:, :LANE].astype(jnp.float32))[:ROW_DEV]
+    diag = jnp.sum(own_t * own_t, axis=1, keepdims=True)
+    rows_t = xwt[:, lanes(s * toks, toks)]
+    nloc[...] = OFF_SCALE * (
+        jnp.dot(rows_t, z_hi, preferred_element_type=jnp.float32)
+        + jnp.dot(rows_t, z_lo, preferred_element_type=jnp.float32)
+    )
+    nloc[mine, :] = nloc[mine, :] + (1.0 - OFF_SCALE) * diag * w_t
+    copy_a = remote(
+        nloc.at[:, lanes(ot * half, half)], n_a, a_sem.at[0], a_sem.at[1], (m, b, ot)
+    )
+    copy_a.start()
+    sent.append(copy_a)
+
+    gram_chunk(1)
+    copy_a.wait_recv()
+    n_s[...] = nloc[:, lanes(t * half, half)] + n_a[...]
+    stage_c = []
+    for k in range(1, nb):
+        bp = lax.rem(b + k, nb)
+        cp = remote(
+            n_s.at[ds(bp * ROW_DEV, ROW_DEV), :], n_c.at[k],
+            c_send.at[k], c_recv.at[k], (m, bp, t),
+        )
+        cp.start()
+        stage_c.append(cp)
+    sent += stage_c
+    forward_chunk(0)
+
+    for c in range(2, len(chunks)):
+        gram_chunk(c)
+        forward_chunk(c - 1)
+    total = n_s[mine, :]
+    for k, cp in enumerate(stage_c):
+        cp.wait_recv()
+        total = total + n_c[k + 1]
+    n_t[...] = total
+    copy_d = remote(n_t, n_d, d_sem.at[0], d_sem.at[1], (om, b, t))
+    copy_d.start()
+    sent.append(copy_d)
+    forward_chunk(len(chunks) - 1)
+
     copy_d.wait_recv()
+    num[...] = n_t[...] + n_d[...]
     for cp in forwards:
         cp.wait_recv()
     for cp in sent + forwards:
         cp.wait_send()
     for c, (off, width) in enumerate(chunks):
-        src = g.at[ds(b * ROW_DEV, ROW_DEV), off:off + width]
+        src = g.at[mine, off:off + width]
         dst = den.at[:, lanes(base + off, width)]
         cp = remote(src, dst, p_send.at[c, 0], p_recv.at[c, slot], (m, b, ot))
         pl.when(owner != t)(cp.wait_send)
@@ -217,8 +237,8 @@
     cols = w.shape[0]
     rows = nb * ROW_DEV
     quarter = span // 4
-    first = (quarter // LANE + 1) // 2 * LANE
-    chunks = [(0, first), (first, quarter - first)]
+    step = -(-quarter // (4 * LANE)) * LANE
+    chunks = [(o, min(step, quarter - o)) for o in range(0, quarter, step)]
     nc = len(chunks)
     dma = pltpu.SemaphoreType.DMA
     f32, bf16 = jnp.float32, jnp.bfloat16
@@ -228,7 +248,7 @@
             jax.ShapeDtypeStruct((ROW_DEV, nb * span // 2), f32),
             jax.ShapeDtypeStruct((ROW_DEV, cols // 2), f32),
         ),
-        in_specs=[pl.BlockSpec(memory_space=pl.ANY)] * 2,
+        in_specs=[pl.BlockSpec(memory_space=pltpu.HBM)] * 2,
         out_specs=(pl.BlockSpec(memory_space=pltpu.VMEM),) * 2,
         scratch_shapes=[
             pltpu.VMEM((toks, span), bf16),
@@ -239,21 +259,21 @@
             pltpu.VMEM((rows, cols), f32),
             pltpu.VMEM((rows, cols // 2), f32),
             pltpu.VMEM((rows, cols // 2), f32),
-            pltpu.VMEM((rows, cols // 4), f32),
-            pltpu.VMEM((rows, cols // 4), f32),
-            pltpu.VMEM((nb, ROW_DEV, cols // 4), f32),
+            pltpu.VMEM((nb, ROW_DEV, cols // 2), f32),
+            pltpu.VMEM((ROW_DEV, cols // 2), f32),
+            pltpu.VMEM((ROW_DEV, cols // 2), f32),
             dma((3,)),
             dma((nc, 3)), dma((nc, 3)),
-            dma((nb,)), dma((nb,)),
-            dma((3,)), dma((3,)),
+            dma((2, nb)), dma((2, nb)),
+            dma((2,)), dma((2,)),
             dma((nc, nb)), dma((nc, nb)),
             dma((nc, nb)), dma((nc, nb)),
-            dma((2,)), dma((2,)),
+            dma((2,)),
             dma((nb,)), dma((nb,)),
-            dma((2,)),
+            dma((4,)),
         ],
         compiler_params=pltpu.CompilerParams(
-            collective_id=0, has_side_effects=True, vmem_limit_bytes=40 * 1024 * 1024
+            collective_id=0, has_side_effects=True, vmem_limit_bytes=62 * 1024 * 1024
         ),
         cost_estimate=pl.CostEstimate(
             flops=2 * toks * span * cols + 2 * rows * quarter * 4 * toks,

time: 62.5 us -> 53.3 us (0.85); the launches traced: 61.5 us -> 53.1 us
  Pallas kernels: 55.8 us -> 49 us
  local copies, waits for them, and re-layouts: 5.06 us -> 3.47 us
    pallas_call x1, Pallas kernels: 55.8 us -> 49 us  [fused(): pl.pallas_call(functools.partial(kernel, nb, chunks), out_shape=(jax.Shap...]
    unnamed x6 -> x4, local copies, waits for them, and re-layouts: 5.06 us -> 3.47 us
where the time goes in v2:
time: 53.3 us; the launch traced here: 53.1 us
  Pallas kernels  49 us (92%)
  local copies, waits for them, and re-layouts  3.47 us (7%)
  between operations  0.65 us (1%)
    pallas_call x1, Pallas kernels, fused(): pl.pallas_call(functools.partial(kernel, nb, chunks), out_shape=(jax.Shap...  49 us
    unnamed x4, local copies, waits for them, and re-layouts  3.47 us

profile of v2, /device:TPU:1, one launch (start us, length us, event | category | flops | bytes accessed | tf_op | source)
XLA Modules:
  0.0 53.1 jit_solution(10556999674879249669)
XLA Ops:
  0.6 49.0 %shard_map.41 = (f32[32,14336]{1,0:T(8,128)}, f32[32,256]{1,0:T(8,128)}) custom-call(bf16[128,3584]{1,0:T(8,128)(2,1)} %bitcast.3, bf16[512,3584]{1,0:T(8,128)(2,1)} %bitcast.2), custom_call_target="tpu_custom_call" | custom-call | flops 704643072 | bytes 6422528 | tf_op jit(solution)/shard_map/pallas_call | solution.py:245
  49.7 0.0 copy-start
  49.7 2.9 %copy.6 = f32[32,14336]{1,0:T(8,128)} copy(f32[32,14336]{1,0:T(8,128)} %get-tuple-element.4) | data formatting | bytes 3670016
  52.5 0.0 copy-done
  52.5 0.6 %copy.7 = f32[32,256]{1,0:T(8,128)} copy(f32[32,256]{1,0:T(8,128)S(1)} %copy-done) | data formatting | bytes 65536
Async XLA Ops:
  49.7 2.9 %copy-start = (f32[32,256]{1,0:T(8,128)S(1)}, f32[32,256]{1,0:T(8,128)}, u32[]{:S(2)}) copy-start(f32[32,256]{1,0:T(8,128)} %get-tuple-element.5) | copy-start | bytes 98308

commit v3 on v2

--- a/solution.py
+++ b/solution.py
@@ -24,7 +24,7 @@
 def kernel(
     nb, chunks,
     x_hbm, w_hbm, den, num,
-    xv, wv, xq, xwt, g, nloc, n_a, n_s, n_c, n_t, n_d,
+    xv, wv, xq, xwt, g, nloc, n_a, n_s, n_y, n_u, n_c, n_t, n_d,
     ld, xs_send, xs_recv, s1_send, s1_recv, s2_send, s2_recv,
     p_send, p_recv, f_send, f_recv, a_sem, c_send, c_recv, d_sem,
 ):
@@ -116,7 +116,8 @@
 
     owner = b // per_half
     base = lax.rem(b, per_half) * span + s * quarter
-    slot = lax.rem(b, per_half) * 2 + t
+    place = lax.rem(b, per_half)
+    slot = place * 2 + t
     half = cols // 2
 
     def gram_chunk(c):
@@ -137,8 +138,9 @@
             g[:, off:off + width] = jnp.where(on_diag, gram, OFF_SCALE * gram)
         else:
             g[:, off:off + width] = OFF_SCALE * gram
-        for k in list(range(1, nb)) + [0]:
-            bp = lax.rem(b + k, nb)
+        for k in list(range(per_half, nb)) + list(range(1, per_half)) + [0]:
+            side = 1 - owner if k >= per_half else owner
+            bp = side * per_half + lax.rem(place + k + 1 if k >= per_half else place + k, per_half)
             src = g.at[ds(bp * ROW_DEV, ROW_DEV), off:off + width]
             dst = den.at[:, lanes(base + off, width)]
             cp = remote(src, dst, p_send.at[c, k], p_recv.at[c, slot], (m, bp, owner))
@@ -155,7 +157,7 @@
     def forward_chunk(c):
         off, width = chunks[c]
         for j in range(nb):
-            i = lax.rem(lax.rem(b, per_half) + (per_half - j // 2), per_half)
+            i = lax.rem(place + (2 * per_half - j // 2 - 1), per_half)
             core = j % 2
             where = i * 2 + core
             came = den.at[:, lanes(i * span + (m * 2 + core) * quarter + off, width)]
@@ -166,58 +168,73 @@
             cp.start()
             forwards.append(cp)
 
+    pairs, zb, y = nb // 2, b // 2, lax.rem(b, 2)
+    copy_a = remote(
+        nloc.at[:, lanes(ot * half, half)], n_a, a_sem.at[0], a_sem.at[1], (m, b, ot)
+    )
+    copy_y = remote(
+        n_s.at[:, 1 - y], n_y, a_sem.at[2], a_sem.at[3], (m, b + 1 - 2 * y, t)
+    )
+    stage_c = []
+    for k in range(1, pairs):
+        zp = lax.rem(zb + k, pairs)
+        stage_c.append(remote(
+            n_u.at[zp], n_c.at[k], c_send.at[k], c_recv.at[k], (m, zp * 2 + y, t)
+        ))
+    copy_d = remote(n_t, n_d, d_sem.at[0], d_sem.at[1], (om, b, t))
+
+    def product():
+        load_w.wait()
+        z = lax.dot_general(
+            xv[...], wv[...], (((1,), (1,)), ((), ())),
+            preferred_element_type=jnp.float32,
+        )
+        z_hi = z.astype(jnp.bfloat16)
+        z_lo = (z - z_hi.astype(jnp.float32)).astype(jnp.bfloat16)
+        w_t = jnp.transpose(wv[:, :LANE].astype(jnp.float32))[:ROW_DEV]
+        diag = jnp.sum(own_t * own_t, axis=1, keepdims=True)
+        rows_t = xwt[:, lanes(s * toks, toks)]
+        nloc[...] = OFF_SCALE * (
+            jnp.dot(rows_t, z_hi, preferred_element_type=jnp.float32)
+            + jnp.dot(rows_t, z_lo, preferred_element_type=jnp.float32)
+        )
+        nloc[mine, :] = nloc[mine, :] + (1.0 - OFF_SCALE) * diag * w_t
+        copy_a.start()
+
+    def over_pair():
+        copy_a.wait_recv()
+        summed = nloc[:, lanes(t * half, half)] + n_a[...]
+        n_s[...] = summed.reshape(n_s.shape)
+        copy_y.start()
+
+    def over_blocks():
+        copy_y.wait_recv()
+        n_u[...] = n_s[:, y] + n_y[...]
+        for cp in stage_c:
+            cp.start()
+
+    def over_models():
+        total = n_u[zb]
+        for k, cp in enumerate(stage_c):
+            cp.wait_recv()
+            total = total + n_c[k + 1]
+        n_t[...] = total
+        copy_d.start()
+
     load_q.wait()
     for cp in stage2:
         cp.wait_recv()
-    gram_chunk(0)
-
-    load_w.wait()
-    z = lax.dot_general(
-        xv[...], wv[...], (((1,), (1,)), ((), ())), preferred_element_type=jnp.float32
-    )
-    z_hi = z.astype(jnp.bfloat16)
-    z_lo = (z - z_hi.astype(jnp.float32)).astype(jnp.bfloat16)
-    w_t = jnp.transpose(wv[:, :LANE].astype(jnp.float32))[:ROW_DEV]
-    diag = jnp.sum(own_t * own_t, axis=1, keepdims=True)
-    rows_t = xwt[:, lanes(s * toks, toks)]
-    nloc[...] = OFF_SCALE * (
-        jnp.dot(rows_t, z_hi, preferred_element_type=jnp.float32)
-        + jnp.dot(rows_t, z_lo, preferred_element_type=jnp.float32)
-    )
-    nloc[mine, :] = nloc[mine, :] + (1.0 - OFF_SCALE) * diag * w_t
-    copy_a = remote(
-        nloc.at[:, lanes(ot * half, half)], n_a, a_sem.at[0], a_sem.at[1], (m, b, ot)
-    )
-    copy_a.start()
-    sent.append(copy_a)
-
-    gram_chunk(1)
-    copy_a.wait_recv()
-    n_s[...] = nloc[:, lanes(t * half, half)] + n_a[...]
-    stage_c = []
-    for k in range(1, nb):
-        bp = lax.rem(b + k, nb)
-        cp = remote(
-            n_s.at[ds(bp * ROW_DEV, ROW_DEV), :], n_c.at[k],
-            c_send.at[k], c_recv.at[k], (m, bp, t),
-        )
-        cp.start()
-        stage_c.append(cp)
-    sent += stage_c
-    forward_chunk(0)
-
-    for c in range(2, len(chunks)):
+    last = len(chunks) - 1
+    for c in range(last + 1):
         gram_chunk(c)
-        forward_chunk(c - 1)
-    total = n_s[mine, :]
-    for k, cp in enumerate(stage_c):
-        cp.wait_recv()
-        total = total + n_c[k + 1]
-    n_t[...] = total
-    copy_d = remote(n_t, n_d, d_sem.at[0], d_sem.at[1], (om, b, t))
-    copy_d.start()
-    sent.append(copy_d)
-    forward_chunk(len(chunks) - 1)
+        for at, step in enumerate((product, over_pair, over_blocks)):
+            if c == min(at, last):
+                step()
+    for c in range(last + 1):
+        forward_chunk(c)
+        if c == min(1, last):
+            over_models()
+    sent += [copy_a, copy_y, copy_d] + stage_c
 
     copy_d.wait_recv()
     num[...] = n_t[...] + n_d[...]
@@ -258,8 +275,10 @@
             pltpu.VMEM((rows, quarter), f32),
             pltpu.VMEM((rows, cols), f32),
             pltpu.VMEM((rows, cols // 2), f32),
-            pltpu.VMEM((rows, cols // 2), f32),
-            pltpu.VMEM((nb, ROW_DEV, cols // 2), f32),
+            pltpu.VMEM((nb // 2, 2, ROW_DEV, cols // 2), f32),
+            pltpu.VMEM((nb // 2, ROW_DEV, cols // 2), f32),
+            pltpu.VMEM((nb // 2, ROW_DEV, cols // 2), f32),
+            pltpu.VMEM((nb // 2, ROW_DEV, cols // 2), f32),
             pltpu.VMEM((ROW_DEV, cols // 2), f32),
             pltpu.VMEM((ROW_DEV, cols // 2), f32),
             dma((3,)),
@@ -268,19 +287,22 @@
             dma((2,)), dma((2,)),
             dma((nc, nb)), dma((nc, nb)),
             dma((nc, nb)), dma((nc, nb)),
-            dma((2,)),
-            dma((nb,)), dma((nb,)),
+            dma((4,)),
+            dma((nb // 2,)), dma((nb // 2,)),
             dma((4,)),
         ],
         compiler_params=pltpu.CompilerParams(
-            collective_id=0, has_side_effects=True, vmem_limit_bytes=62 * 1024 * 1024
+            collective_id=0, has_side_effects=True, vmem_limit_bytes=40 * 1024 * 1024
         ),
         cost_estimate=pl.CostEstimate(
             flops=2 * toks * span * cols + 2 * rows * quarter * 4 * toks,
             bytes_accessed=2 * (toks + cols) * span + 2 * ROW_DEV * nb * span,
             transcendentals=0,
         ),
-    )(x, w)
+    )(
+        pltpu.with_memory_space_constraint(x, pltpu.HBM),
+        pltpu.with_memory_space_constraint(w, pltpu.HBM),
+    )
 
 
 def general(x, w, din):

time: 53.3 us -> 54 us (1.013)
  Pallas kernels: 49 us -> 51 us
  local copies, waits for them, and re-layouts: 3.47 us -> 1.85 us
    pallas_call x1, Pallas kernels: 49 us -> 51 us  [fused(): pl.pallas_call(functools.partial(kernel, nb, chunks), out_shape=(jax.Shap...]
    unnamed x4 -> x2, local copies, waits for them, and re-layouts: 3.47 us -> 1.85 us
where the time goes in v3:
time: 54 us; the launch traced here: 53.5 us
  Pallas kernels  51 us (94%)
  local copies, waits for them, and re-layouts  1.85 us (3%)
  between operations  0.64 us (1%)
    pallas_call x1, Pallas kernels, fused(): pl.pallas_call(functools.partial(kernel, nb, chunks), out_shape=(jax.Shap...  51 us
    unnamed x2, local copies, waits for them, and re-layouts  1.85 us

profile of v3, /device:TPU:1, one launch (start us, length us, event | category | flops | bytes accessed | tf_op | source)
XLA Modules:
  0.0 53.5 jit_solution(10340880728459390158)
XLA Ops:
  0.6 51.0 %shard_map.41 = (f32[32,14336]{1,0:T(8,128)S(1)}, f32[32,256]{1,0:T(8,128)S(1)}) custom-call(bf16[128,3584]{1,0:T(8,128)(2,1)} %bitcast.3, bf16[512,3584]{1,0:T(8,128)(2,1)} %bitcast.2), custom_call_target="tpu_custom_call" | custom-call | flops 704643072 | bytes 6422528 | tf_op jit(solution)/shard_map/pallas_call | solution.py:262
  51.7 1.2 %copy.6 = f32[32,14336]{1,0:T(8,128)} copy(f32[32,14336]{1,0:T(8,128)S(1)} %get-tuple-element.4) | data formatting | bytes 3670016
  52.9 0.6 %copy.7 = f32[32,256]{1,0:T(8,128)} copy(f32[32,256]{1,0:T(8,128)S(1)} %get-tuple-element.5) | data formatting | bytes 65536

commit v4 on v3

--- a/solution.py
+++ b/solution.py
@@ -78,8 +78,11 @@
             ))
         exchange.append(copies)
         sent += copies
-    for cp in exchange[0]:
-        cp.start()
+    def send_exchange(c):
+        for cp in exchange[c]:
+            cp.start()
+
+    send_exchange(0)
 
     load_x.wait()
     mine = ds(b * ROW_DEV, ROW_DEV)
@@ -102,8 +105,7 @@
         for cp in copies:
             cp.start()
         stage1.append(copies)
-    for cp in exchange[1]:
-        cp.start()
+    send_exchange(1)
     stage2 = []
     for r in range(2):
         for cp in stage1[r]:
@@ -119,14 +121,14 @@
     place = lax.rem(b, per_half)
     slot = place * 2 + t
     half = cols // 2
+    order = [k for r in range(1, per_half) for k in (per_half + r - 1, r)] + [nb - 1, 0]
 
     def gram_chunk(c):
         off, width = chunks[c]
         for cp in exchange[c]:
             cp.wait_recv()
         if c + 2 < len(chunks):
-            for cp in exchange[c + 2]:
-                cp.start()
+            send_exchange(c + 2)
         gram = jnp.dot(
             xwt[...], xq[:, off:off + width], preferred_element_type=jnp.float32
         )
@@ -138,7 +140,7 @@
             g[:, off:off + width] = jnp.where(on_diag, gram, OFF_SCALE * gram)
         else:
             g[:, off:off + width] = OFF_SCALE * gram
-        for k in list(range(per_half, nb)) + list(range(1, per_half)) + [0]:
+        for k in order:
             side = 1 - owner if k >= per_half else owner
             bp = side * per_half + lax.rem(place + k + 1 if k >= per_half else place + k, per_half)
             src = g.at[ds(bp * ROW_DEV, ROW_DEV), off:off + width]
@@ -230,10 +232,10 @@
         for at, step in enumerate((product, over_pair, over_blocks)):
             if c == min(at, last):
                 step()
-    for c in range(last + 1):
-        forward_chunk(c)
-        if c == min(1, last):
-            over_models()
+        if c:
+            forward_chunk(c - 1)
+    over_models()
+    forward_chunk(last)
     sent += [copy_a, copy_y, copy_d] + stage_c
 
     copy_d.wait_recv()

time: 54 us -> 47.8 us (0.89)
  Pallas kernels: 51 us -> 45.2 us
    pallas_call x1, Pallas kernels: 51 us -> 45.2 us  [fused(): pl.pallas_call(functools.partial(kernel, nb, chunks), out_shape=(jax.Shap...]
where the time goes in v4:
time: 47.8 us; the launch traced here: 47.7 us
  Pallas kernels  45.2 us (95%)
  local copies, waits for them, and re-layouts  1.85 us (4%)
  between operations  0.64 us (1%)
    pallas_call x1, Pallas kernels, fused(): pl.pallas_call(functools.partial(kernel, nb, chunks), out_shape=(jax.Shap...  45.2 us
    unnamed x2, local copies, waits for them, and re-layouts  1.85 us

profile of v4, /device:TPU:1, one launch (start us, length us, event | category | flops | bytes accessed | tf_op | source)
XLA Modules:
  0.0 47.7 jit_solution(9816138156413799991)
XLA Ops:
  0.6 45.2 %shard_map.41 = (f32[32,14336]{1,0:T(8,128)S(1)}, f32[32,256]{1,0:T(8,128)S(1)}) custom-call(bf16[128,3584]{1,0:T(8,128)(2,1)} %bitcast.3, bf16[512,3584]{1,0:T(8,128)(2,1)} %bitcast.2), custom_call_target="tpu_custom_call" | custom-call | flops 704643072 | bytes 6422528 | tf_op jit(solution)/shard_map/pallas_call | solution.py:264
  45.8 1.2 %copy.6 = f32[32,14336]{1,0:T(8,128)} copy(f32[32,14336]{1,0:T(8,128)S(1)} %get-tuple-element.4) | data formatting | bytes 3670016
  47.1 0.6 %copy.7 = f32[32,256]{1,0:T(8,128)} copy(f32[32,256]{1,0:T(8,128)S(1)} %get-tuple-element.5) | data formatting | bytes 65536
